TPU v7x, 256 devices: a whole 4x4x8 slice. The times are simulated.
256 devices in a mesh: vert: 128 (over z, y, x), qcol: 2 (over core).
Axes of the slice: x: 4, y: 4, z: 8, core: 2. Of those that a mesh axis runs over, the one named last changes fastest.
Arguments:
- descriptors: bfloat16 [262144, 2048], P('vert'), may hold values from -0.8984375 to 0.8984375
- queries: bfloat16 [512, 2048], P('qcol', 'vert'), may hold values from -0.8984375 to 0.8984375
- tiles: bfloat16 [6144, 128, 128], P('vert'), may hold values from 0 to 1, as said below
- tile_cols: int32 [128, 3, 16], replicated, may hold values from 0 to 15, as said below
- part_size: int32 [128], replicated, may hold values from 1024 to 2048, as said below
Outputs:
- ranking: float32 [262144, 512], P('vert', 'qcol')
- residual: float32 [262144, 512], P('vert', 'qcol')
Inputs may be any that keep to these rules, and one draw needn't show every extreme that they name: For each part d and slot j, tile_cols[d, j, :] is a permutation of 0 to 15. `part_size`: some part has exactly 2048 live vertices and some exactly 1024. tiles are sparse and nonnegative; every row and every column of B sums to at most 1.01.
All inputs are finite; a program needn't handle non-finite values.
Results may differ from a plain program's by a relative error of at most 0.0003.
Values may be sent and summed in bfloat16 or wider, within the bound.
A program may use at most 128 MiB of HBM per device.

v0:
```python
import jax
import jax.numpy as jnp
from jax import lax
from jax.sharding import PartitionSpec as P

ITERS = 2


def padded(block, sides, width):
    for axis, dim in sides:
        count = lax.axis_size(axis)
        forward = [(i, i + 1) for i in range(count - 1)]
        forward.append((count - 1, 0))
        backward = [(target, source) for source, target in forward]
        low = lax.ppermute(
            lax.slice_in_dim(block, block.shape[dim] - width, None, axis=dim), axis, forward
        )
        high = lax.ppermute(lax.slice_in_dim(block, 0, width, axis=dim), axis, backward)
        block = jnp.concatenate([low, block, high], axis=dim)
    return block


def shifted(x, axis, by):
    peers = lax.axis_size(axis)
    return lax.ppermute(x, axis, [(i, (i + by) % peers) for i in range(peers)])


def transposed(blocks_slot, rows3, cols_row):
    moved = jnp.einsum("rba,rbq->raq", blocks_slot, rows3, precision=lax.Precision.HIGHEST)
    return moved[jnp.argsort(cols_row)]


def body(descriptors, queries, tiles, tile_cols, part_size):
    rows = descriptors.shape[0]
    qdev = queries.shape[0]
    tile = tiles.shape[1]
    rtiles = rows // tile
    slots = tiles.shape[0] // rtiles
    here = lax.axis_index("vert")
    sims = lax.dot_general(
        descriptors,
        lax.all_gather(queries, "vert", axis=1, tiled=True),
        (((1,), (1,)), ((), ())),
        preferred_element_type=jnp.float32,
    )
    live_count = lax.dynamic_index_in_dim(part_size, here, 0, keepdims=False)
    live = (lax.iota(jnp.int32, rows) < live_count).astype(jnp.float32)[:, None]
    seeds = live * jnp.maximum(sims, 0.0) ** 3
    blocks = tiles.astype(jnp.float32).reshape(slots, rtiles, tile, tile)
    own_cols = lax.dynamic_index_in_dim(tile_cols, here, 0, keepdims=False)

    def squares(values):
        return lax.psum(jnp.sum(values * values, axis=0), "vert")

    ranking = jnp.zeros_like(seeds)
    residual = seeds
    direction = seeds
    norm_now = squares(residual)
    for step in range(ITERS):
        widened = padded(direction, (("vert", 0),), rows)
        forward = jnp.zeros((rtiles, tile, qdev), jnp.float32)
        for slot in range(slots):
            source = widened[slot * rows : (slot + 1) * rows].reshape(rtiles, tile, qdev)
            picked = source[own_cols[slot]]
            forward = forward + jnp.einsum(
                "rab,rbq->raq", blocks[slot], picked, precision=lax.Precision.HIGHEST
            )
        own3 = direction.reshape(rtiles, tile, qdev)
        middle = transposed(blocks[1], own3, own_cols[1])
        toward_low = transposed(blocks[0], own3, own_cols[0])
        toward_high = transposed(blocks[slots - 1], own3, own_cols[slots - 1])
        back = middle + shifted(toward_low, "vert", -1) + shifted(toward_high, "vert", 1)
        both = (forward + back).reshape(rows, qdev)
        image = direction - 0.99 * live * (0.5 * both)
        curve = lax.psum(jnp.sum(direction * image, axis=0), "vert")
        alpha = norm_now / curve
        ranking = ranking + alpha[None, :] * direction
        residual = residual - alpha[None, :] * image
        norm_next = squares(residual)
        direction = residual + (norm_next / norm_now)[None, :] * direction
        norm_now = norm_next
    return (ranking, residual)


def solution(mesh):
    placed = (P("vert", None), P("qcol", "vert"), P("vert", None, None), P(), P())
    return jax.shard_map(
        body,
        mesh=mesh,
        in_specs=placed,
        out_specs=(P("vert", "qcol"), P("vert", "qcol")),
        check_vma=False,
    )
```

profile of v0, /device:TPU:0, one launch (start us, length us, event | category | flops | bytes accessed | tf_op | source)
XLA Modules:
  0.0 1348.9 jit_solution(10652084589290533953)
XLA Ops:
  14.6 100.5 %all-gather.2.cloned.1.call-done = bf16[256,2048]{0,1:T(8,128)(2,1)} async-done(((bf16[256,16]{0,1:T(8,128)(2,1)}), bf16[256,2048]{0,1:T(8,128)(2,1)}) %all-gather.2.cloned.1.call-update) | async-done | bytes 1048592 | tf_op jit(solution)/shard_map/all_gather | solution.py:42
  115.1 6.1 fusion
  122.6 6.1 collective-permute-start.1
  128.7 4.3 convolution_bitcast_fusion.4
  140.9 4.3 convolution_bitcast_fusion.3
  153.1 4.3 convolution_bitcast_fusion.5
  165.9 4.1 fusion.17
  170.0 5.3 collective-permute-done
  175.4 3.6 gather_fusion
  179.0 3.7 gather_fusion.2
  185.7 28.8 %collective-permute-done.2 = f32[16,128,256]{2,1,0:T(8,128)} collective-permute-done((f32[16,128,256]{2,1,0:T(8,128)}, f32[16,128,256]{2,1,0:T(8,128)}, u32[]{:S(2)}, u32[]{:S(2)}) %collective-permute-start.2) | collective-permute-done | bytes 2097184 | tf_op jit(solution)/shard_map/ppermute | solution.py:25
  215.2 5.1 bitcast_add_fusion.1
  221.7 349.4 %all-reduce = (f32[256]{0:T(256)S(1)}, f32[256]{0:T(256)S(1)}) all-reduce(f32[256]{0:T(256)S(1)} %get-tuple-element.9, f32[256]{0:T(256)S(1)} %get-tuple-element.8), channel_id=1, replica_groups=mesh['vert'=128,'qcol'=2] {'vert'}, use_global_device_ids=true, to_apply=%region_1.2 | all-reduce | flops 512 | bytes 4096 | tf_op jit(solution)/shard_map/psum | solution.py:53
  573.1 343.0 %psum.30 = f32[256]{0:T(256)S(1)} all-reduce(f32[256]{0:T(256)S(1)} %multiply_reduce_fusion.1), channel_id=1, replica_groups=mesh['vert'=128,'qcol'=2] {'vert'}, use_global_device_ids=true, to_apply=%region_8.9 | all-reduce | flops 256 | bytes 2048 | tf_op jit(solution)/shard_map/psum | solution.py:53
  921.5 5.5 collective-permute-start.5
  927.0 4.9 convolution_bitcast_fusion.1
  938.4 5.0 convolution_bitcast_fusion
  955.6 5.0 convolution_bitcast_fusion.2
  963.5 3.6 gather_fusion.9
  967.1 4.1 fusion.14
  971.3 3.6 gather_fusion.6
  981.9 5.1 bitcast_add_fusion
  990.3 347.1 %psum.31 = f32[256]{0:T(256)S(1)} all-reduce(f32[256]{0:T(256)S(1)} %multiply_reduce_fusion), channel_id=1, replica_groups=mesh['vert'=128,'qcol'=2] {'vert'}, use_global_device_ids=true, to_apply=%region_10.11 | all-reduce | flops 256 | bytes 2048 | tf_op jit(solution)/shard_map/psum | solution.py:75
  1337.5 4.6 multiply_subtract_fusion
  (70 shorter events, 77.5 us)
Async XLA Ops:
  7.2 107.9 %all-gather.2.cloned.1.call-start = ((), (), s32[]{:S(2)}) async-start(), calls=%async_computation | async-start | bytes 1056768 | tf_op jit(solution)/shard_map/all_gather | solution.py:42
  121.2 54.2 %collective-permute-start = (f32[2048,256]{1,0:T(8,128)S(1)}, f32[2048,256]{1,0:T(8,128)}, u32[]{:S(2)}, u32[]{:S(2)}) collective-permute-start(f32[2048,256]{1,0:T(8,128)S(1)} %fusion), channel_id=1, source_target_pairs={{0,2},{2,4},{4,6},{6,8},{8,10},{10,12},{12,14},{14,16},{16,18},{18... | collective-permute-start | bytes 6291464 | tf_op jit(solution)/shard_map/ppermute | solution.py:15
  122.6 56.4 %collective-permute-start.1 = (f32[2048,256]{1,0:T(8,128)S(1)}, f32[2048,256]{1,0:T(8,128)}, u32[]{:S(2)}, u32[]{:S(2)}) collective-permute-start(f32[2048,256]{1,0:T(8,128)S(1)} %fusion), channel_id=1, source_target_pairs={{2,0},{4,2},{6,4},{8,6},{10,8},{12,10},{14,12},{16,14},{18,16},{20... | collective-permute-start | bytes 6291464 | tf_op jit(solution)/shard_map/ppermute | solution.py:18
  139.5 74.9 %collective-permute-start.2 = (f32[16,128,256]{2,1,0:T(8,128)}, f32[16,128,256]{2,1,0:T(8,128)}, u32[]{:S(2)}, u32[]{:S(2)}) collective-permute-start(f32[16,128,256]{2,1,0:T(8,128)} %gather_fusion.4), channel_id=1, source_target_pairs={{0,254},{2,0},{4,2},{6,4},{8,6},{10,8},{12,10},{14,12},{16,14},{18... | collective-permute-start | bytes 6291464 | tf_op jit(solution)/shard_map/ppermute | solution.py:25
  151.6 63.5 %collective-permute-start.3 = (f32[16,128,256]{2,1,0:T(8,128)}, f32[16,128,256]{2,1,0:T(8,128)}, u32[]{:S(2)}, u32[]{:S(2)}) collective-permute-start(f32[16,128,256]{2,1,0:T(8,128)} %gather_fusion.5), channel_id=1, source_target_pairs={{0,2},{2,4},{4,6},{6,8},{8,10},{10,12},{12,14},{14,16},{16,18},{18... | collective-permute-start | bytes 6291464 | tf_op jit(solution)/shard_map/ppermute | solution.py:25
  182.7 32.5 %copy-start.4 = (f32[16,128,256]{2,1,0:T(8,128)S(1)}, f32[16,128,256]{2,1,0:T(8,128)}, u32[]{:S(2)}) copy-start(f32[16,128,256]{2,1,0:T(8,128)} %gather_fusion.3) | copy-start | bytes 6291460
  182.7 32.5 %copy-start.5 = (f32[16,256,128]{1,2,0:T(8,128)S(1)}, f32[16,256,128]{1,2,0:T(8,128)}, u32[]{:S(2)}) copy-start(f32[16,256,128]{1,2,0:T(8,128)} %fusion.17) | copy-start | bytes 6291460
  220.3 1.4 copy-start
  919.5 51.7 %collective-permute-start.4 = (f32[2048,256]{1,0:T(8,128)}, f32[2048,256]{1,0:T(8,128)}, u32[]{:S(2)}, u32[]{:S(2)}) collective-permute-start(f32[2048,256]{1,0:T(8,128)} %multiply_add_fusion.1), channel_id=1, source_target_pairs={{0,2},{2,4},{4,6},{6,8},{8,10},{10,12},{12,14},{14,16},{16,18},{18... | collective-permute-start | bytes 6291464 | tf_op jit(solution)/shard_map/ppermute | solution.py:15
  921.5 53.4 %collective-permute-start.5 = (f32[2048,256]{1,0:T(8,128)}, f32[2048,256]{1,0:T(8,128)}, u32[]{:S(2)}, u32[]{:S(2)}) collective-permute-start(f32[2048,256]{1,0:T(8,128)} %multiply_add_fusion.1), channel_id=1, source_target_pairs={{2,0},{4,2},{6,4},{8,6},{10,8},{12,10},{14,12},{16,14},{18,16},{20... | collective-permute-start | bytes 6291464 | tf_op jit(solution)/shard_map/ppermute | solution.py:18
  938.4 43.0 %collective-permute-start.6 = (f32[16,128,256]{2,1,0:T(8,128)}, f32[16,128,256]{2,1,0:T(8,128)}, u32[]{:S(2)}, u32[]{:S(2)}) collective-permute-start(f32[16,128,256]{2,1,0:T(8,128)} %gather_fusion.10), channel_id=1, source_target_pairs={{0,254},{2,0},{4,2},{6,4},{8,6},{10,8},{12,10},{14,12},{16,14},{18... | collective-permute-start | bytes 6291464 | tf_op jit(solution)/shard_map/ppermute | solution.py:25
  949.9 32.0 %collective-permute-start.7 = (f32[16,128,256]{2,1,0:T(8,128)}, f32[16,128,256]{2,1,0:T(8,128)}, u32[]{:S(2)}, u32[]{:S(2)}) collective-permute-start(f32[16,128,256]{2,1,0:T(8,128)} %gather_fusion.11), channel_id=1, source_target_pairs={{0,2},{2,4},{4,6},{6,8},{8,10},{10,12},{12,14},{14,16},{16,18},{18... | collective-permute-start | bytes 6291464 | tf_op jit(solution)/shard_map/ppermute | solution.py:25
  978.5 3.5 copy-start.2
  978.5 3.5 copy-start.3
  987.1 1.3 copy-start.1
Sparse Core Ops, SparseCore 0:
  11.4 103.6 all-gather.1
where the time goes:
time: 1350 us
  blocking collectives  1040 us (77%)
  waiting for transfers between devices  136 us (10%)
  local copies, waits for them, and re-layouts  63.5 us (5%)
  matrix products  58.4 us (4%)
  starting transfers between devices  19.1 us (1%)
  other arithmetic  17.7 us (1%)
  between operations  14.2 us (1%)
    psum x2, blocking collectives, squares(): return lax.psum(jnp.sum(values * values, axis=0), 'vert')  692 us
    psum x1, blocking collectives, body(): curve = lax.psum(jnp.sum(direction * image, axis=0), 'vert')  347 us
    all_gather x1, waiting for transfers between devices, body(): lax.all_gather(queries, 'vert', axis=1, tiled=True)  100 us
    ppermute x4, waiting for transfers between devices, shifted(): return lax.ppermute(x, axis, [(i, (i + by) % peers) for i in range(peers)])  30 us
    dot_general x6, matrix products, transposed(): jnp.einsum('rba,rbq->raq', blocks_slot, rows3, precision=lax.Precision.HI...  27.8 us
  transfers between devices with their start and end apart: 9, of which 5 were waited for; matrix products, arithmetic and copies ran while one was open for 8% of the time, Pallas kernels for 0%

commit v1 on v0

--- a/solution.py
+++ b/solution.py
@@ -4,6 +4,15 @@
 from jax.sharding import PartitionSpec as P
 
 ITERS = 2
+attach_types = lambda x_part, ax_name: jnp.concatenate(
+    lax.all_to_all(
+        jnp.stack([x_part] * lax.axis_size(ax_name), axis=0),
+        axis_name=ax_name,
+        split_axis=0,
+        concat_axis=0,
+    ),
+    axis=1,
+)
 
 
 def padded(block, sides, width):
@@ -39,7 +48,7 @@
     here = lax.axis_index("vert")
     sims = lax.dot_general(
         descriptors,
-        lax.all_gather(queries, "vert", axis=1, tiled=True),
+        attach_types(queries, "vert"),
         (((1,), (1,)), ((), ())),
         preferred_element_type=jnp.float32,
     )

time: 1350 us -> 1290 us (0.956)
  waiting for transfers between devices: 136 us -> 61.7 us
  starting transfers between devices: 19.1 us -> 33.9 us
    all_gather x1 -> x0, waiting for transfers between devices: 100 us -> none  [body(): lax.all_gather(queries, 'vert', axis=1, tiled=True)]
    all_to_all x0 -> x1, waiting for transfers between devices: none -> 25.8 us  [lax.all_to_all(jnp.stack([x_part] * lax.axis_size(ax_name), axis=0), axis...]
    all_to_all x0 -> x1, starting transfers between devices: none -> 14.1 us  [lax.all_to_all(jnp.stack([x_part] * lax.axis_size(ax_name), axis=0), axis...]
where the time goes in v1:
time: 1290 us; the launch traced here: 1280 us
  blocking collectives  1040 us (81%)
  local copies, waits for them, and re-layouts  63.9 us (5%)
  waiting for transfers between devices  61.7 us (5%)
  matrix products  58.2 us (5%)
  starting transfers between devices  33.9 us (3%)
  other arithmetic  17.6 us (1%)
    psum x2, blocking collectives, squares(): return lax.psum(jnp.sum(values * values, axis=0), 'vert')  692 us
    psum x1, blocking collectives, body(): curve = lax.psum(jnp.sum(direction * image, axis=0), 'vert')  347 us
    ppermute x4, waiting for transfers between devices, shifted(): return lax.ppermute(x, axis, [(i, (i + by) % peers) for i in range(peers)])  31 us
    dot_general x6, matrix products, transposed(): jnp.einsum('rba,rbq->raq', blocks_slot, rows3, precision=lax.Precision.HI...  27.8 us
    all_to_all x1, waiting for transfers between devices, lax.all_to_all(jnp.stack([x_part] * lax.axis_size(ax_name), axis=0), axis...  25.8 us
  transfers between devices with their start and end apart: 9, of which 5 were waited for; matrix products, arithmetic and copies ran while one was open for 8% of the time, Pallas kernels for 0%

profile of v1, /device:TPU:0, one launch (start us, length us, event | category | flops | bytes accessed | tf_op | source)
XLA Modules:
  0.0 1276.0 jit_solution(10983612727115683058)
XLA Ops:
  2.4 14.1 %all-to-all-start = ((bf16[128,256,16]{1,2,0:T(8,128)(2,1)}), bf16[128,256,16]{1,2,0:T(8,128)(2,1)S(1)}, u32[]{:S(2)}, u32[]{:S(2)}) async-start(bf16[128,256,16]{1,2,0:T(8,128)(2,1)} %stack.2), calls=%async_computation | async-start | bytes 2097152 | tf_op jit(solution)/shard_map/all_to_all | solution.py:8
  21.8 25.8 %all-to-all-done = bf16[128,256,16]{1,2,0:T(8,128)(2,1)S(1)} async-done(((bf16[128,256,16]{1,2,0:T(8,128)(2,1)}), bf16[128,256,16]{1,2,0:T(8,128)(2,1)S(1)}, u32[]{:S(2)}, u32[]{:S(2)}) %all-to-all-start) | async-done | bytes 1048608 | tf_op jit(solution)/shard_map/all_to_all | solution.py:8
  47.6 5.8 fusion
  54.2 6.8 collective-permute-start.1
  61.0 4.3 convolution_bitcast_fusion.4
  71.8 4.3 convolution_bitcast_fusion.3
  85.8 4.3 convolution_bitcast_fusion.5
  98.6 4.1 fusion.17
  102.8 4.9 collective-permute-done
  107.7 3.6 gather_fusion
  111.3 3.7 gather_fusion.2
  118.0 29.8 %collective-permute-done.2 = f32[16,128,256]{2,1,0:T(8,128)} collective-permute-done((f32[16,128,256]{2,1,0:T(8,128)}, f32[16,128,256]{2,1,0:T(8,128)}, u32[]{:S(2)}, u32[]{:S(2)}) %collective-permute-start.2) | collective-permute-done | bytes 2097184 | tf_op jit(solution)/shard_map/ppermute | solution.py:34
  148.6 5.1 bitcast_add_fusion.1
  155.0 349.3 %all-reduce = (f32[256]{0:T(256)S(1)}, f32[256]{0:T(256)S(1)}) all-reduce(f32[256]{0:T(256)S(1)} %get-tuple-element.9, f32[256]{0:T(256)S(1)} %get-tuple-element.8), channel_id=1, replica_groups=mesh['vert'=128,'qcol'=2] {'vert'}, use_global_device_ids=true, to_apply=%region_1.2 | all-reduce | flops 512 | bytes 4096 | tf_op jit(solution)/shard_map/psum | solution.py:62
  506.4 343.0 %psum.30 = f32[256]{0:T(256)S(1)} all-reduce(f32[256]{0:T(256)S(1)} %multiply_reduce_fusion.1), channel_id=1, replica_groups=mesh['vert'=128,'qcol'=2] {'vert'}, use_global_device_ids=true, to_apply=%region_8.9 | all-reduce | flops 256 | bytes 2048 | tf_op jit(solution)/shard_map/psum | solution.py:62
  854.8 5.7 collective-permute-start.5
  860.5 5.0 convolution_bitcast_fusion.1
  871.9 4.9 convolution_bitcast_fusion
  889.3 5.0 convolution_bitcast_fusion.2
  897.2 3.6 gather_fusion.9
  900.8 4.1 fusion.14
  915.6 5.1 bitcast_add_fusion
  924.0 347.2 %psum.31 = f32[256]{0:T(256)S(1)} all-reduce(f32[256]{0:T(256)S(1)} %multiply_reduce_fusion), channel_id=1, replica_groups=mesh['vert'=128,'qcol'=2] {'vert'}, use_global_device_ids=true, to_apply=%region_10.11 | all-reduce | flops 256 | bytes 2048 | tf_op jit(solution)/shard_map/psum | solution.py:84
  1271.2 4.6 multiply_subtract_fusion
  (74 shorter events, 80.6 us)
Async XLA Ops:
  0.6 15.8 %copy-start.7 = (s32[128]{0:T(128)S(1)}, s32[128]{0:T(128)}, u32[]{:S(2)}) copy-start(s32[128]{0:T(128)} %param.9) | copy-start | bytes 1540
  0.6 16.5 %copy-start.6 = (s32[128,3,16]{0,2,1:T(8,128)S(1)}, s32[128,3,16]{0,2,1:T(8,128)}, u32[]{:S(2)}) copy-start(s32[128,3,16]{0,2,1:T(8,128)} %param.8) | copy-start | bytes 73732
  2.4 45.2 %all-to-all-start = ((bf16[128,256,16]{1,2,0:T(8,128)(2,1)}), bf16[128,256,16]{1,2,0:T(8,128)(2,1)S(1)}, u32[]{:S(2)}, u32[]{:S(2)}) async-start(bf16[128,256,16]{1,2,0:T(8,128)(2,1)} %stack.2), calls=%async_computation | async-start | bytes 2097152 | tf_op jit(solution)/shard_map/all_to_all | solution.py:8
  53.5 54.2 %collective-permute-start = (f32[2048,256]{1,0:T(8,128)S(1)}, f32[2048,256]{1,0:T(8,128)}, u32[]{:S(2)}, u32[]{:S(2)}) collective-permute-start(f32[2048,256]{1,0:T(8,128)S(1)} %fusion), channel_id=1, source_target_pairs={{0,2},{2,4},{4,6},{6,8},{8,10},{10,12},{12,14},{14,16},{16,18},{18... | collective-permute-start | bytes 6291464 | tf_op jit(solution)/shard_map/ppermute | solution.py:24
  54.2 57.1 %collective-permute-start.1 = (f32[2048,256]{1,0:T(8,128)S(1)}, f32[2048,256]{1,0:T(8,128)}, u32[]{:S(2)}, u32[]{:S(2)}) collective-permute-start(f32[2048,256]{1,0:T(8,128)S(1)} %fusion), channel_id=1, source_target_pairs={{2,0},{4,2},{6,4},{8,6},{10,8},{12,10},{14,12},{16,14},{18,16},{20... | collective-permute-start | bytes 6291464 | tf_op jit(solution)/shard_map/ppermute | solution.py:27
  71.8 76.0 %collective-permute-start.2 = (f32[16,128,256]{2,1,0:T(8,128)}, f32[16,128,256]{2,1,0:T(8,128)}, u32[]{:S(2)}, u32[]{:S(2)}) collective-permute-start(f32[16,128,256]{2,1,0:T(8,128)} %gather_fusion.4), channel_id=1, source_target_pairs={{0,254},{2,0},{4,2},{6,4},{8,6},{10,8},{12,10},{14,12},{16,14},{18... | collective-permute-start | bytes 6291464 | tf_op jit(solution)/shard_map/ppermute | solution.py:34
  82.6 66.0 %collective-permute-start.3 = (f32[16,128,256]{2,1,0:T(8,128)}, f32[16,128,256]{2,1,0:T(8,128)}, u32[]{:S(2)}, u32[]{:S(2)}) collective-permute-start(f32[16,128,256]{2,1,0:T(8,128)} %gather_fusion.5), channel_id=1, source_target_pairs={{0,2},{2,4},{4,6},{6,8},{8,10},{10,12},{12,14},{14,16},{16,18},{18... | collective-permute-start | bytes 6291464 | tf_op jit(solution)/shard_map/ppermute | solution.py:34
  115.0 33.6 %copy-start.4 = (f32[16,128,256]{2,1,0:T(8,128)S(1)}, f32[16,128,256]{2,1,0:T(8,128)}, u32[]{:S(2)}) copy-start(f32[16,128,256]{2,1,0:T(8,128)} %gather_fusion.3) | copy-start | bytes 6291460
  115.0 33.6 %copy-start.5 = (f32[16,256,128]{1,2,0:T(8,128)S(1)}, f32[16,256,128]{1,2,0:T(8,128)}, u32[]{:S(2)}) copy-start(f32[16,256,128]{1,2,0:T(8,128)} %fusion.17) | copy-start | bytes 6291460
  153.7 1.4 copy-start
  852.9 52.1 %collective-permute-start.4 = (f32[2048,256]{1,0:T(8,128)}, f32[2048,256]{1,0:T(8,128)}, u32[]{:S(2)}, u32[]{:S(2)}) collective-permute-start(f32[2048,256]{1,0:T(8,128)} %multiply_add_fusion.1), channel_id=1, source_target_pairs={{0,2},{2,4},{4,6},{6,8},{8,10},{10,12},{12,14},{14,16},{16,18},{18... | collective-permute-start | bytes 6291464 | tf_op jit(solution)/shard_map/ppermute | solution.py:24
  854.8 53.7 %collective-permute-start.5 = (f32[2048,256]{1,0:T(8,128)}, f32[2048,256]{1,0:T(8,128)}, u32[]{:S(2)}, u32[]{:S(2)}) collective-permute-start(f32[2048,256]{1,0:T(8,128)} %multiply_add_fusion.1), channel_id=1, source_target_pairs={{2,0},{4,2},{6,4},{8,6},{10,8},{12,10},{14,12},{16,14},{18,16},{20... | collective-permute-start | bytes 6291464 | tf_op jit(solution)/shard_map/ppermute | solution.py:27
  871.9 43.2 %collective-permute-start.6 = (f32[16,128,256]{2,1,0:T(8,128)}, f32[16,128,256]{2,1,0:T(8,128)}, u32[]{:S(2)}, u32[]{:S(2)}) collective-permute-start(f32[16,128,256]{2,1,0:T(8,128)} %gather_fusion.10), channel_id=1, source_target_pairs={{0,254},{2,0},{4,2},{6,4},{8,6},{10,8},{12,10},{14,12},{16,14},{18... | collective-permute-start | bytes 6291464 | tf_op jit(solution)/shard_map/ppermute | solution.py:34
  883.4 32.1 %collective-permute-start.7 = (f32[16,128,256]{2,1,0:T(8,128)}, f32[16,128,256]{2,1,0:T(8,128)}, u32[]{:S(2)}, u32[]{:S(2)}) collective-permute-start(f32[16,128,256]{2,1,0:T(8,128)} %gather_fusion.11), channel_id=1, source_target_pairs={{0,2},{2,4},{4,6},{6,8},{8,10},{10,12},{12,14},{14,16},{16,18},{18... | collective-permute-start | bytes 6291464 | tf_op jit(solution)/shard_map/ppermute | solution.py:34
  912.1 3.5 copy-start.2
  912.1 3.5 copy-start.3
  920.7 1.3 copy-start.1
